TPU v7x, 32 devices: a whole 2x2x4 slice. The times are simulated.
32 devices in a mesh: expert: 8 (over z, core), fsdp: 4 (over y, x).
Axes of the slice: x: 2, y: 2, z: 4, core: 2. Of those that a mesh axis runs over, the one named last changes fastest.
Arguments:
- tokens: bfloat16 [16384, 1024], P(('expert', 'fsdp')), may hold values from -6 to 6
- norm_one: bfloat16 [1024], P('fsdp'), may hold values from 0.25 to 1.75
- query_weight: bfloat16 [1024, 1024], P('fsdp'), may hold values from -0.25 to 0.25
- key_projection_matrix: bfloat16 [1024, 512], P('fsdp'), may hold values from -0.1875 to 0.1875
- value_projection_matrix: bfloat16 [1024, 512], P('fsdp'), may hold values from -0.1875 to 0.1875
- out_weight: bfloat16 [1024, 1024], P('fsdp'), may hold values from -0.5 to 0.5
- norm_two: bfloat16 [1024], P('fsdp'), may hold values from 0.25 to 1.75
- router_weight: bfloat16 [1024, 32], P('fsdp'), may hold values from -0.09375 to 0.09375
- gate_weight: bfloat16 [32, 1024, 512], P('expert'), may hold values from -0.1875 to 0.1875
- up_weight: bfloat16 [32, 1024, 512], P('expert'), may hold values from -0.1875 to 0.1875
- down_weight: bfloat16 [32, 512, 1024], P('expert'), may hold values from -0.75 to 0.75
- routes: int32 [16384, 8], P(('expert', 'fsdp')), may hold values from 0 to 31, all different within a row; in each aligned block of 512 rows (0 to 511, 512 to 1023, ...) at most 192 rows name the same one
- out_grad: bfloat16 [16384, 1024], P(('expert', 'fsdp')), may hold values from -6 to 6
Outputs:
- block_out: bfloat16 [16384, 1024], P(('expert', 'fsdp'))
- input_grad: float32 [16384, 1024], P(('expert', 'fsdp'))
- norm_one_grad: float32 [1024], P('fsdp')
- query_grad: float32 [1024, 1024], P('fsdp')
- key_grad: float32 [1024, 512], P('fsdp')
- value_grad: float32 [1024, 512], P('fsdp')
- out_proj_grad: float32 [1024, 1024], P('fsdp')
- norm_two_grad: float32 [1024], P('fsdp')
- router_grad: float32 [1024, 32], P('fsdp')
- gate_grad: float32 [32, 1024, 512], P('expert')
- up_grad: float32 [32, 1024, 512], P('expert')
- down_grad: float32 [32, 512, 1024], P('expert')
Inputs may be any that keep to these rules, and one draw needn't show every extreme that they name: `routes`: each row names 8 different experts. Within the 512 rows of one device (aligned blocks) no expert is named by more than 192 rows, and in every draw some expert is named by exactly 192 rows of some block.
All inputs are finite; a program needn't handle non-finite values.
Results may differ from a plain program's by a relative error of at most 0.023.
Values may be sent and summed in bfloat16 or wider, within the bound.
A program may use at most 320 MiB of HBM per device.

v0:
```python
import jax
import jax.numpy as jnp
from jax import lax
from jax.sharding import PartitionSpec as P

MODEL_WIDTH = 1024
QUERY_HEADS = 16
KEY_VALUE_HEADS = 8
HEAD_WIDTH = 64
EXPERTS = 32
TOPK = 8
CAP = 192


EPSILON = 1e-05
THETA = 10000.0
NEGATIVE = -1e30
HIGH_PRECISION = lax.Precision.HIGHEST


def rms_scale(values, gain):
    return values * lax.rsqrt(jnp.mean(values * values, axis=-1, keepdims=True) + EPSILON) * gain


def rope_tables(length, head_size):
    half_size = head_size // 2
    freqs = jnp.power(THETA, -2.0 * jnp.arange(half_size).astype(jnp.float32) / head_size)
    angles = jnp.arange(length).astype(jnp.float32)[:, None] * freqs[None, :]
    return (jnp.cos(angles), jnp.sin(angles))


def apply_rotation_heads(values, cosine_table, sine_table, direction):
    half_size = values.shape[-1] // 2
    lead_half = values[..., :half_size]
    tail_half = values[..., half_size:]
    cos_part = cosine_table[:, None, :]
    sin_part = sine_table[:, None, :] * direction
    return jnp.concatenate(
        [lead_half * cos_part - tail_half * sin_part, tail_half * cos_part + lead_half * sin_part],
        axis=-1,
    )


def inner_rows(left_mat, right_mat):
    return lax.dot_general(
        left_mat, right_mat, (((0,), (0,)), ((), ())), preferred_element_type=jnp.float32
    )


def outer_cols(left_mat, right_mat):
    return lax.dot_general(
        left_mat, right_mat, (((1,), (1,)), ((), ())), preferred_element_type=jnp.float32
    )


def masked_scores(query_rotated, key_rotated):
    length = query_rotated.shape[0]
    attention_scores = jnp.einsum(
        "mhwo,pho->hwmp", query_rotated, key_rotated, preferred_element_type=jnp.float32
    ) * HEAD_WIDTH ** (-0.5)
    causal = jnp.arange(length)[:, None] >= jnp.arange(length)[None, :]
    return jnp.where(causal, attention_scores, NEGATIVE)


def on_device(
    tokens,
    norm_one,
    query_weight,
    key_projection_matrix,
    value_projection_matrix,
    out_weight,
    norm_two,
    router_weight,
    gate_weight,
    up_weight,
    down_weight,
    routes,
    out_grad,
):
    n_expert = lax.axis_size("expert")
    token_rows = tokens.shape[0]
    exp_local = gate_weight.shape[0]
    query_group_width = QUERY_HEADS // KEY_VALUE_HEADS
    attn_gain, query_full, key_full, value_full, outproj_full, moe_gain, router_full = (
        lax.all_gather(norm_one, "fsdp", axis=0, tiled=True),
        lax.all_gather(query_weight, "fsdp", axis=0, tiled=True),
        lax.all_gather(key_projection_matrix, "fsdp", axis=0, tiled=True),
        lax.all_gather(value_projection_matrix, "fsdp", axis=0, tiled=True),
        lax.all_gather(out_weight, "fsdp", axis=0, tiled=True),
        lax.all_gather(norm_two, "fsdp", axis=0, tiled=True),
        lax.all_gather(router_weight, "fsdp", axis=0, tiled=True),
    )
    x_float = tokens.astype(jnp.float32)
    gain_first = attn_gain.astype(jnp.float32)
    normed_one, norm_one_back = jax.vjp(rms_scale, x_float, gain_first)
    normed_low = normed_one.astype(jnp.bfloat16)
    query_pre = jnp.dot(normed_low, query_full, preferred_element_type=jnp.float32)
    key_before_rotation = jnp.dot(normed_low, key_full, preferred_element_type=jnp.float32)
    value_reduced = jnp.dot(normed_low, value_full, preferred_element_type=jnp.float32).astype(
        jnp.bfloat16
    )
    cosine_table, sine_table = rope_tables(token_rows, HEAD_WIDTH)
    query_rotated = apply_rotation_heads(
        query_pre.reshape(token_rows, QUERY_HEADS, HEAD_WIDTH), cosine_table, sine_table, 1.0
    ).astype(jnp.bfloat16)
    query_rotated = query_rotated.reshape(
        token_rows, KEY_VALUE_HEADS, query_group_width, HEAD_WIDTH
    )
    key_rotated = apply_rotation_heads(
        key_before_rotation.reshape(token_rows, KEY_VALUE_HEADS, HEAD_WIDTH),
        cosine_table,
        sine_table,
        1.0,
    ).astype(jnp.bfloat16)
    value_per_head = value_reduced.reshape(token_rows, KEY_VALUE_HEADS, HEAD_WIDTH)
    masked = masked_scores(query_rotated, key_rotated)
    row_top = jnp.max(masked, axis=-1, keepdims=True)
    expo = jnp.exp(masked - row_top)
    row_total = jnp.sum(expo, axis=-1, keepdims=True)
    log_total = row_top + jnp.log(row_total)
    probability_reduced = (expo / row_total).astype(jnp.bfloat16)
    attn_heads = jnp.einsum(
        "nfea,anm->enfm", probability_reduced, value_per_head, preferred_element_type=jnp.float32
    )
    attn_low = attn_heads.reshape(token_rows, QUERY_HEADS * HEAD_WIDTH).astype(jnp.bfloat16)
    attn_proj = jnp.dot(attn_low, outproj_full, preferred_element_type=jnp.float32)
    resid_one = x_float + attn_proj
    gain_second = moe_gain.astype(jnp.float32)
    normed_two, norm_two_back = jax.vjp(rms_scale, resid_one, gain_second)
    moe_input = normed_two.astype(jnp.bfloat16)
    logits = jnp.dot(moe_input, router_full, preferred_element_type=jnp.float32)
    route_pick = (routes[:, :, None] == jnp.arange(EXPERTS)[None, None, :]).astype(jnp.float32)
    chosen = jnp.sum(route_pick * logits[:, None, :], axis=-1)
    chosen_top = jnp.max(chosen, axis=-1, keepdims=True)
    chosen_exp = jnp.exp(chosen - chosen_top)
    gates = chosen_exp / jnp.sum(chosen_exp, axis=-1, keepdims=True)
    flat_route = routes.reshape(-1)
    pick = (flat_route[:, None] == jnp.arange(EXPERTS)[None, :]).astype(jnp.int32)
    running = jnp.cumsum(pick, axis=0) - 1
    slot_index = jnp.sum(running * pick, axis=1)
    send_rows = (
        jnp.zeros((EXPERTS, CAP, MODEL_WIDTH), jnp.bfloat16)
        .at[flat_route, slot_index]
        .set(jnp.repeat(moe_input, TOPK, axis=0))
    )
    send_rows = send_rows.reshape(n_expert, exp_local, CAP, MODEL_WIDTH)
    arrived_rows = lax.all_to_all(send_rows, "expert", split_axis=0, concat_axis=0, tiled=True)
    gate_part = jnp.einsum(
        "nesd,edf->nesf", arrived_rows, gate_weight, preferred_element_type=jnp.float32
    )
    up_part = jnp.einsum(
        "nesd,edf->nesf", arrived_rows, up_weight, preferred_element_type=jnp.float32
    )
    hidden_part = (gate_part * jax.nn.sigmoid(gate_part) * up_part).astype(jnp.bfloat16)
    expert_out = jnp.einsum(
        "nesf,efd->nesd", hidden_part, down_weight, preferred_element_type=jnp.float32
    ).astype(jnp.bfloat16)
    returned_part = lax.all_to_all(expert_out, "expert", split_axis=0, concat_axis=0, tiled=True)
    back_rows = (
        returned_part.reshape(EXPERTS, CAP, MODEL_WIDTH)[flat_route, slot_index]
        .astype(jnp.float32)
        .reshape(token_rows, TOPK, MODEL_WIDTH)
    )
    moe_sum = jnp.sum(gates[:, :, None] * back_rows, axis=1)
    block_out = (resid_one + moe_sum).astype(jnp.bfloat16)
    grad_float = out_grad.astype(jnp.float32)
    gate_score = jnp.sum(back_rows * grad_float[:, None, :], axis=-1)
    chosen_grad = gates * (gate_score - jnp.sum(gates * gate_score, axis=-1, keepdims=True))
    logit_grad = jnp.sum(chosen_grad[:, :, None] * route_pick, axis=1)
    router_local = jnp.dot(moe_input.astype(jnp.float32).T, logit_grad, precision=HIGH_PRECISION)
    router_back = jnp.dot(logit_grad, router_full.astype(jnp.float32).T, precision=HIGH_PRECISION)
    slot_grad = (
        (gates[:, :, None] * grad_float[:, None, :])
        .astype(jnp.bfloat16)
        .reshape(token_rows * TOPK, MODEL_WIDTH)
    )
    grad_send = (
        jnp.zeros((EXPERTS, CAP, MODEL_WIDTH), jnp.bfloat16)
        .at[flat_route, slot_index]
        .set(slot_grad)
    )
    grad_send = grad_send.reshape(n_expert, exp_local, CAP, MODEL_WIDTH)
    grad_arrived = lax.all_to_all(grad_send, "expert", split_axis=0, concat_axis=0, tiled=True)
    sigma = jax.nn.sigmoid(gate_part)
    silu_value = gate_part * sigma
    hidden = (silu_value * up_part).astype(jnp.bfloat16)
    down_local = jnp.einsum(
        "nesf,nesd->efd", hidden, grad_arrived, preferred_element_type=jnp.float32
    )
    hidden_grad = jnp.einsum(
        "nesd,efd->nesf", grad_arrived, down_weight, preferred_element_type=jnp.float32
    )
    gate_low = (hidden_grad * up_part * sigma * (1.0 + gate_part * (1.0 - sigma))).astype(
        jnp.bfloat16
    )
    up_low = (hidden_grad * silu_value).astype(jnp.bfloat16)
    gate_local = jnp.einsum(
        "nesd,nesf->edf", arrived_rows, gate_low, preferred_element_type=jnp.float32
    )
    up_local = jnp.einsum(
        "nesd,nesf->edf", arrived_rows, up_low, preferred_element_type=jnp.float32
    )
    row_grad = jnp.einsum(
        "nesf,edf->nesd", gate_low, gate_weight, preferred_element_type=jnp.float32
    )
    row_grad = (
        row_grad
        + jnp.einsum("nesf,edf->nesd", up_low, up_weight, preferred_element_type=jnp.float32)
    ).astype(jnp.bfloat16)
    row_back = lax.all_to_all(row_grad, "expert", split_axis=0, concat_axis=0, tiled=True)
    gate_sum, up_sum, down_sum = (
        lax.psum(gate_local.astype(jnp.bfloat16), "fsdp").astype(jnp.float32),
        lax.psum(up_local.astype(jnp.bfloat16), "fsdp").astype(jnp.float32),
        lax.psum(down_local.astype(jnp.bfloat16), "fsdp").astype(jnp.float32),
    )
    home_rows = (
        row_back.reshape(EXPERTS, CAP, MODEL_WIDTH)[flat_route, slot_index]
        .astype(jnp.float32)
        .reshape(token_rows, TOPK, MODEL_WIDTH)
    )
    normed_two_grad = jnp.sum(home_rows, axis=1) + router_back
    resid_from_norm, gain_two_grad = norm_two_back(normed_two_grad)
    resid_grad = grad_float + resid_from_norm
    proj_low = resid_grad.astype(jnp.bfloat16)
    outproj_local = inner_rows(attn_low, proj_low)
    head_outputs_gradient = (
        outer_cols(proj_low, outproj_full)
        .astype(jnp.bfloat16)
        .reshape(token_rows, KEY_VALUE_HEADS, query_group_width, HEAD_WIDTH)
    )
    attention_probability = jnp.exp(masked_scores(query_rotated, key_rotated) - log_total)
    probability_recomputed = attention_probability.astype(jnp.bfloat16)
    value_reduced_gradient = jnp.einsum(
        "jfek,ejfa->kja",
        probability_recomputed,
        head_outputs_gradient,
        preferred_element_type=jnp.float32,
    )
    value_reduced_gradient = value_reduced_gradient.reshape(
        token_rows, KEY_VALUE_HEADS * HEAD_WIDTH
    ).astype(jnp.bfloat16)
    prob_grad = jnp.einsum(
        "mhwo,pho->hwmp", head_outputs_gradient, value_per_head, preferred_element_type=jnp.float32
    )
    scores_gradient = (
        attention_probability
        * (prob_grad - jnp.sum(attention_probability * prob_grad, axis=-1, keepdims=True))
    ).astype(jnp.bfloat16)
    query_rot_grad = jnp.einsum(
        "nfea,anm->enfm", scores_gradient, key_rotated, preferred_element_type=jnp.float32
    ) * HEAD_WIDTH ** (-0.5)
    key_rot_grad = jnp.einsum(
        "jfek,ejfa->kja", scores_gradient, query_rotated, preferred_element_type=jnp.float32
    ) * HEAD_WIDTH ** (-0.5)
    query_low_grad = (
        apply_rotation_heads(
            query_rot_grad.reshape(token_rows, QUERY_HEADS, HEAD_WIDTH),
            cosine_table,
            sine_table,
            -1.0,
        )
        .reshape(token_rows, QUERY_HEADS * HEAD_WIDTH)
        .astype(jnp.bfloat16)
    )
    key_low_grad = (
        apply_rotation_heads(key_rot_grad, cosine_table, sine_table, -1.0)
        .reshape(token_rows, KEY_VALUE_HEADS * HEAD_WIDTH)
        .astype(jnp.bfloat16)
    )
    query_local = inner_rows(normed_low, query_low_grad)
    key_local = inner_rows(normed_low, key_low_grad)
    value_local = inner_rows(normed_low, value_reduced_gradient)
    normed_one_grad = (
        outer_cols(query_low_grad, query_full)
        + outer_cols(key_low_grad, key_full)
        + outer_cols(value_reduced_gradient, value_full)
    )
    x_from_norm, gain_one_grad = norm_one_back(normed_one_grad)
    input_grad = resid_grad + x_from_norm
    gain_a, query_a, key_a, value_a, outproj_a, gain_b, router_a = (
        lax.psum_scatter(
            gain_one_grad.astype(jnp.bfloat16), "fsdp", scatter_dimension=0, tiled=True
        ).astype(jnp.float32),
        lax.psum_scatter(
            query_local.astype(jnp.bfloat16), "fsdp", scatter_dimension=0, tiled=True
        ).astype(jnp.float32),
        lax.psum_scatter(
            key_local.astype(jnp.bfloat16), "fsdp", scatter_dimension=0, tiled=True
        ).astype(jnp.float32),
        lax.psum_scatter(
            value_local.astype(jnp.bfloat16), "fsdp", scatter_dimension=0, tiled=True
        ).astype(jnp.float32),
        lax.psum_scatter(
            outproj_local.astype(jnp.bfloat16), "fsdp", scatter_dimension=0, tiled=True
        ).astype(jnp.float32),
        lax.psum_scatter(
            gain_two_grad.astype(jnp.bfloat16), "fsdp", scatter_dimension=0, tiled=True
        ).astype(jnp.float32),
        lax.psum_scatter(
            router_local.astype(jnp.bfloat16), "fsdp", scatter_dimension=0, tiled=True
        ).astype(jnp.float32),
    )
    gain_c, query_c, key_c, value_c, outproj_c, gain_d, router_c = (
        lax.psum(gain_a.astype(jnp.bfloat16), "expert").astype(jnp.float32),
        lax.psum(query_a.astype(jnp.bfloat16), "expert").astype(jnp.float32),
        lax.psum(key_a.astype(jnp.bfloat16), "expert").astype(jnp.float32),
        lax.psum(value_a.astype(jnp.bfloat16), "expert").astype(jnp.float32),
        lax.psum(outproj_a.astype(jnp.bfloat16), "expert").astype(jnp.float32),
        lax.psum(gain_b.astype(jnp.bfloat16), "expert").astype(jnp.float32),
        lax.psum(router_a.astype(jnp.bfloat16), "expert").astype(jnp.float32),
    )
    return (
        block_out,
        input_grad,
        gain_c,
        query_c,
        key_c,
        value_c,
        outproj_c,
        gain_d,
        router_c,
        gate_sum,
        up_sum,
        down_sum,
    )


def solution(mesh):
    return jax.shard_map(
        on_device,
        mesh=mesh,
        in_specs=(
            P(("expert", "fsdp"), None),
            P("fsdp"),
            P("fsdp", None),
            P("fsdp", None),
            P("fsdp", None),
            P("fsdp", None),
            P("fsdp"),
            P("fsdp", None),
            P("expert", None, None),
            P("expert", None, None),
            P("expert", None, None),
            P(("expert", "fsdp"), None),
            P(("expert", "fsdp"), None),
        ),
        out_specs=(
            P(("expert", "fsdp"), None),
            P(("expert", "fsdp"), None),
            P("fsdp"),
            P("fsdp", None),
            P("fsdp", None),
            P("fsdp", None),
            P("fsdp", None),
            P("fsdp"),
            P("fsdp", None),
            P("expert", None, None),
            P("expert", None, None),
            P("expert", None, None),
        ),
        check_vma=False,
    )
```

profile of v0, /device:TPU:0, one launch (start us, length us, event | category | flops | bytes accessed | tf_op | source)
XLA Modules:
  0.0 1694.8 jit_solution(2109424608668054652)
XLA Ops:
  46.9 21.0 %all-gather.7.cloned.1.call-done = bf16[1024,512]{1,0:T(8,128)(2,1)} async-done(((bf16[256,512]{1,0:T(8,128)(2,1)}), bf16[1024,512]{1,0:T(8,128)(2,1)}) %all-gather.7.cloned.1.call-update) | async-done | bytes 1048592 | tf_op jit(solution)/shard_map/all_gather | solution.py:88
  70.0 35.1 %all-gather.11.cloned.1.call-done = bf16[1024,1024]{1,0:T(8,128)(2,1)} async-done(((bf16[256,1024]{1,0:T(8,128)(2,1)}), bf16[1024,1024]{1,0:T(8,128)(2,1)}) %all-gather.11.cloned.1.call-update) | async-done | bytes 2097168 | tf_op jit(solution)/shard_map/all_gather | solution.py:86
  146.7 25.7 %scatter_custom_fusion = bf16[6144,1024]{1,0:T(8,128)(2,1)} fusion(s32[4096]{0:T(1024)S(1)} %broadcast_select_fusion, bf16[]{:T(256)} %constant.15.clone.1, bf16[512,1024]{1,0:T(8,128)(2,1)S(1)} %multiply_convert_fusion), kind=kCustom, calls=%fused_computation.53 | custom fusion | bytes 13631490
  190.5 27.3 %scatter_custom_fusion.1 = bf16[6144,1024]{1,0:T(8,128)(2,1)} fusion(s32[4096]{0:T(1024)S(1)} %broadcast_select_fusion, f32[512,1024]{1,0:T(8,128)S(1)} %convert_element_type.287, f32[4096]{0:T(1024)S(1)} %div.100, bf16[]{:T(256)} %constant.15.clone.1), kind=kCustom, calls=%fused_computation.49 | custom fusion | flops 8388608 | bytes 14696450
  217.9 233.9 %all-to-all-done = bf16[8,4,192,1024]{3,2,1,0:T(8,128)(2,1)} async-done(((bf16[8,4,192,1024]{3,2,1,0:T(8,128)(2,1)}), bf16[8,4,192,1024]{3,2,1,0:T(8,128)(2,1)}, u32[]{:S(2)}, u32[]{:S(2)}) %all-to-all-start) | async-done | bytes 12582944 | tf_op jit(solution)/shard_map/all_to_all | solution.py:147
  457.3 13.7 fusion.22
  470.9 12.3 fusion.24
  483.2 247.8 %all-to-all-done.2 = bf16[8,4,192,1024]{3,2,1,0:T(8,128)(2,1)} async-done(((bf16[8,4,192,1024]{3,2,1,0:T(8,128)(2,1)}), bf16[8,4,192,1024]{3,2,1,0:T(8,128)(2,1)}, u32[]{:S(2)}, u32[]{:S(2)}) %all-to-all-start.2) | async-done | bytes 12582944 | tf_op jit(solution)/shard_map/all_to_all | solution.py:183
  731.0 25.6 %fusion.12 = (bf16[8,4,192,512]{3,2,0,1:T(8,128)(2,1)}, bf16[8,4,192,512]{3,2,0,1:T(8,128)(2,1)}, bf16[8,4,192,512]{3,2,0,1:T(8,128)(2,1)}) fusion(f32[4,8,192,512]{3,2,1,0:T(8,128)} %fusion.24, f32[4,8,192,512]{3,2,1,0:T(8,128)} %fusion.22, bf16[4,512,1024]{2,1,0:T(8,128)(2,1)} %param.23, bf16[8,4,192,1024]{3,2,1,0:T(8,128)(2,1)} %all-to-all-done.2), kind=kOutput, calls=%fused_computation.29 | convolution fusion | flops 6489636864 | bytes 60817408 | tf_op jit(solution)/shard_map/nesd,efd->nesf/dot_general | solution.py:190
  777.7 15.1 fusion.44
  792.7 17.0 %fusion.8 = bf16[8,4,192,1024]{3,2,0,1:T(8,128)(2,1)} fusion(f32[4,8,192,1024]{3,2,1,0:T(8,128)} %fusion.44, bf16[8,4,192,512]{3,2,0,1:T(8,128)(2,1)} %get-tuple-element.30, bf16[4,1024,512]{2,1,0:T(8,128)(2,1)S(1)} %copy-done.13), kind=kOutput, calls=%fused_computation.23 | convolution fusion | flops 6455033856 | bytes 48234496 | tf_op jit(solution)/shard_map/nesf,edf->nesd/dot_general | solution.py:208
  820.5 230.9 %all-to-all-done.1 = bf16[8,4,192,1024]{3,2,1,0:T(8,128)(2,1)} async-done(((bf16[8,4,192,1024]{3,2,1,0:T(8,128)(2,1)}), bf16[8,4,192,1024]{3,2,1,0:T(8,128)(2,1)}, u32[]{:S(2)}, u32[]{:S(2)}) %all-to-all-start.1) | async-done | bytes 12582944 | tf_op jit(solution)/shard_map/all_to_all | solution.py:158
  1056.8 13.9 bitcast_convert_fusion
  1070.8 13.0 bitcast_convert_fusion.1
  1083.8 11.1 bitcast_convert_fusion.2
  1095.7 81.2 %gather_fusion = bf16[4096,1024]{1,0:T(8,128)(2,1)} fusion(bf16[32,192,1024]{2,1,0:T(8,128)(2,1)} %bitcast.27, s32[4096]{0:T(1024)S(1)} %bitcast.203), kind=kCustom, calls=%fused_computation | custom fusion | bytes 16809984 | tf_op jit(solution)/shard_map/gather | solution.py:160
  1187.7 142.9 %all-to-all-done.3 = bf16[8,4,192,1024]{3,2,1,0:T(8,128)(2,1)} async-done(((bf16[8,4,192,1024]{3,2,1,0:T(8,128)(2,1)}), bf16[8,4,192,1024]{3,2,1,0:T(8,128)(2,1)}, u32[]{:S(2)}, u32[]{:S(2)}) %all-to-all-start.3) | async-done | bytes 12582944 | tf_op jit(solution)/shard_map/all_to_all | solution.py:210
  1330.6 80.9 %gather_fusion.1 = bf16[4096,1024]{1,0:T(8,128)(2,1)} fusion(bf16[32,192,1024]{2,1,0:T(8,128)(2,1)} %bitcast.37, s32[4096]{0:T(1024)S(1)} %bitcast.204), kind=kCustom, calls=%fused_computation.1 | custom fusion | bytes 16809984 | tf_op jit(solution)/shard_map/gather | solution.py:217
  1411.6 12.0 convert_reduce_fusion
  1454.3 12.8 fusion.4
  1511.5 38.2 %reduce-scatter.12.cloned.1.call-done = bf16[256,1024]{1,0:T(8,128)(2,1)} async-done(((bf16[1024,1024]{1,0:T(8,128)(2,1)}), bf16[256,1024]{1,0:T(8,128)(2,1)}) %reduce-scatter.12.cloned.1.call-update) | async-done | bytes 524304 | tf_op jit(solution)/shard_map/reduce_scatter | solution.py:293
  1549.7 38.5 %reduce-scatter.6.cloned.1.call-done = bf16[256,1024]{1,0:T(8,128)(2,1)} async-done(((bf16[1024,1024]{1,0:T(8,128)(2,1)}), bf16[256,1024]{1,0:T(8,128)(2,1)}) %reduce-scatter.6.cloned.1.call-update) | async-done | bytes 524304 | tf_op jit(solution)/shard_map/reduce_scatter | solution.py:284
  1615.0 28.6 %all-reduce.2 = (bf16[256]{0:T(256)(128)(2,1)S(1)}, bf16[256]{0:T(256)(128)(2,1)S(1)}, bf16[256,32]{0,1:T(8,128)(2,1)S(1)}) all-reduce(bf16[256]{0:T(256)(128)(2,1)S(1)} %dynamic-slice.1, bf16[256]{0:T(256)(128)(2,1)S(1)} %dynamic-slice.3, ...), channel_id=1, replica_groups=mesh['expert'=8,'fsdp'=4] {'expert'}, use_global_device_ids=true, to_apply=%region_22.23 | all-reduce | flops 8704 | bytes 34816 | tf_op jit(solution)/shard_map/psum | solution.py:304
  1645.3 34.7 %all-reduce.9.cloned.1.call-done = (bf16[256,1024]{1,0:T(8,128)(2,1)}, bf16[256,512]{1,0:T(8,128)(2,1)}, bf16[256,512]{1,0:T(8,128)(2,1)}, bf16[256,1024]{1,0:T(8,128)(2,1)}) async-done(((bf16[256,1024]{1,0:T(8,128)(2,1)}, bf16[256,512]{1,0:T(8,128)(2,1)}, bf16[256,512]{1,0:T(8,128)(2,1)}, bf16[256,1024]{1,0:T(8,128)(2,1)}), (bf16[256,1024]{1,0:T(8,128)(2,1)}, bf16[256,512]{1,0:T(8,128)(2,1)}, ...) | async-done | bytes 1572880 | tf_op jit(solution)/shard_map/psum | solution.py:305
  (267 shorter events, 265.6 us)
Async XLA Ops:
  7.2 37.4 %all-gather.9.cloned.1.call-start = ((), (), s32[]{:S(2)}) async-start(), calls=%async_computation.10 | async-start | bytes 1310720 | tf_op jit(solution)/shard_map/all_gather | solution.py:87
  7.9 60.0 %all-gather.7.cloned.1.call-start = ((), (), s32[]{:S(2)}) async-start(), calls=%async_computation.9 | async-start | bytes 1310720 | tf_op jit(solution)/shard_map/all_gather | solution.py:88
  8.7 96.4 %all-gather.11.cloned.1.call-start = ((), (), s32[]{:S(2)}) async-start(), calls=%async_computation.11 | async-start | bytes 2621440 | tf_op jit(solution)/shard_map/all_gather | solution.py:86
  9.4 132.7 %all-gather.13.cloned.1.call-start = ((), (), s32[]{:S(2)}) async-start(), calls=%async_computation.12 | async-start | bytes 2621440 | tf_op jit(solution)/shard_map/all_gather | solution.py:89
  14.3 90.8 %copy-start.62 = (f32[512]{0:T(512)}, f32[512]{0:T(512)S(1)}, u32[]{:S(2)}) copy-start(f32[512]{0:T(512)S(1)} %fusion.80) | copy-start | bytes 6148
  23.8 121.9 %copy-start.48 = (f32[4,1,256]{2,1,0:T(1,128)}, f32[4,1,256]{2,1,0:T(1,128)S(1)}, u32[]{:S(2)}) copy-start(f32[4,1,256]{2,1,0:T(1,128)S(1)} %convert_element_type.327) | copy-start | bytes 12292
  31.9 73.2 %copy-start.52 = (f32[4,1,256]{2,1,0:T(1,128)}, f32[4,1,256]{2,1,0:T(1,128)S(1)}, u32[]{:S(2)}) copy-start(f32[4,1,256]{2,1,0:T(1,128)S(1)} %convert_element_type.326) | copy-start | bytes 12292
  172.4 279.3 %all-to-all-start = ((bf16[8,4,192,1024]{3,2,1,0:T(8,128)(2,1)}), bf16[8,4,192,1024]{3,2,1,0:T(8,128)(2,1)}, u32[]{:S(2)}, u32[]{:S(2)}) async-start(bf16[8,4,192,1024]{3,2,1,0:T(8,128)(2,1)} %bitcast.205), calls=%async_computation | async-start | bytes 25165824 | tf_op jit(solution)/shard_map/all_to_all | solution.py:147
  451.7 279.3 %all-to-all-start.2 = ((bf16[8,4,192,1024]{3,2,1,0:T(8,128)(2,1)}), bf16[8,4,192,1024]{3,2,1,0:T(8,128)(2,1)}, u32[]{:S(2)}, u32[]{:S(2)}) async-start(bf16[8,4,192,1024]{3,2,1,0:T(8,128)(2,1)} %bitcast.206), calls=%async_computation.2 | async-start | bytes 25165824 | tf_op jit(solution)/shard_map/all_to_all | solution.py:183
  771.9 279.5 %all-to-all-start.1 = ((bf16[8,4,192,1024]{3,2,1,0:T(8,128)(2,1)}), bf16[8,4,192,1024]{3,2,1,0:T(8,128)(2,1)}, u32[]{:S(2)}, u32[]{:S(2)}) async-start(bf16[8,4,192,1024]{3,2,1,0:T(8,128)(2,1)} %copy.101), calls=%async_computation.1 | async-start | bytes 25165824 | tf_op jit(solution)/shard_map/all_to_all | solution.py:158
  1051.4 279.1 %all-to-all-start.3 = ((bf16[8,4,192,1024]{3,2,1,0:T(8,128)(2,1)}), bf16[8,4,192,1024]{3,2,1,0:T(8,128)(2,1)}, u32[]{:S(2)}, u32[]{:S(2)}) async-start(bf16[8,4,192,1024]{3,2,1,0:T(8,128)(2,1)} %copy.104), calls=%async_computation.3 | async-start | bytes 25165824 | tf_op jit(solution)/shard_map/all_to_all | solution.py:210
  1056.8 430.8 %all-reduce.11.cloned.1.call-start = ((), (), s32[]{:S(2)}) async-start(), calls=%async_computation.19 | async-start | bytes 25165824 | tf_op jit(solution)/shard_map/psum | solution.py:212
  1094.9 415.1 %reduce-scatter.10.cloned.1.call-start = ((), (), s32[]{:S(2)}) async-start(), calls=%async_computation.15 | async-start | bytes 1310720 | tf_op jit(solution)/shard_map/reduce_scatter | solution.py:290
  1095.7 81.3 %copy-start.5 = (f32[512,1024]{1,0:T(8,128)S(1)}, f32[512,1024]{1,0:T(8,128)}, u32[]{:S(2)}) copy-start(f32[512,1024]{1,0:T(8,128)} %copy-done.4) | copy-start | bytes 6291460
  1095.7 81.3 %copy-start.18 = (f32[512,8]{1,0:T(8,128)S(1)}, f32[512,8]{1,0:T(8,128)}, u32[]{:S(2)}) copy-start(f32[512,8]{1,0:T(8,128)} %copy-done.17) | copy-start | bytes 49156
  1330.5 80.9 %copy-start.37 = (f32[512,8]{0,1:T(8,128)S(1)}, f32[512,8]{0,1:T(8,128)}, u32[]{:S(2)}) copy-start(f32[512,8]{0,1:T(8,128)} %copy-done.36) | copy-start | bytes 49156
  1330.5 80.9 %copy-start.51 = (f32[512]{0:T(512)S(1)}, f32[512]{0:T(512)}, u32[]{:S(2)}) copy-start(f32[512]{0:T(512)} %copy-done.50) | copy-start | bytes 6148
  1330.6 80.9 %copy-start.55 = (f32[512]{0:T(512)S(1)}, f32[512]{0:T(512)}, u32[]{:S(2)}) copy-start(f32[512]{0:T(512)} %copy-done.54) | copy-start | bytes 6148
  1330.6 81.0 %copy-start.43 = (s32[512,8]{0,1:T(8,128)S(1)}, s32[512,8]{0,1:T(8,128)}, u32[]{:S(2)}) copy-start(s32[512,8]{0,1:T(8,128)} %param.24) | copy-start | bytes 49156
  1454.2 57.3 %reduce-scatter.8.cloned.1.call-start = ((), (), s32[]{:S(2)}) async-start(), calls=%async_computation.14 | async-start | bytes 1310720 | tf_op jit(solution)/shard_map/reduce_scatter | solution.py:287
  1473.4 76.2 %reduce-scatter.12.cloned.1.call-start = ((), (), s32[]{:S(2)}) async-start(), calls=%async_computation.16 | async-start | bytes 2621440 | tf_op jit(solution)/shard_map/reduce_scatter | solution.py:293
  1477.5 110.7 %reduce-scatter.6.cloned.1.call-start = ((), (), s32[]{:S(2)}) async-start(), calls=%async_computation.13 | async-start | bytes 2621440 | tf_op jit(solution)/shard_map/reduce_scatter | solution.py:284
  1486.2 128.8 %reduce-scatter.14.cloned.1.call-start = ((), (), s32[]{:S(2)}) async-start(), calls=%async_computation.17 | async-start | bytes 81920 | tf_op jit(solution)/shard_map/reduce_scatter | solution.py:299
  1504.8 175.2 %all-reduce.9.cloned.1.call-start = ((), (), s32[]{:S(2)}) async-start(), calls=%async_computation.18 | async-start | bytes 3145728 | tf_op jit(solution)/shard_map/psum | solution.py:305
  (62 other events, 802.1 us)
Sparse Core Ops, SparseCore 0:
  9.9 29.3 all-gather.8
  41.1 26.7 all-gather.6
  69.8 35.2 all-gather.10
  106.8 35.2 all-gather.12
  1095.0 241.2 all-reduce.10
  1454.3 25.6 reduce-scatter.9
  1483.7 27.7 reduce-scatter.7
  1514.4 35.1 reduce-scatter.11
  1552.9 35.1 reduce-scatter.5
  1591.3 23.6 reduce-scatter.13
  1617.8 62.1 all-reduce.8
where the time goes:
time: 1710 us; the launch traced here: 1690 us
  waiting for transfers between devices  1050 us (61%)
  local copies, waits for them, and re-layouts  217 us (13%)
  matrix products  211 us (12%)
  other arithmetic  119 us (7%)
  blocking collectives  63.8 us (4%)
  starting transfers between devices  23 us (1%)
    all_to_all x1, waiting for transfers between devices, on_device(): lax.all_to_all(grad_send, 'expert', split_axis=0, concat_axis=0, tiled=True)  248 us
    all_to_all x1, waiting for transfers between devices, on_device(): lax.all_to_all(send_rows, 'expert', split_axis=0, concat_axis=0, tiled=True)  234 us
    all_to_all x1, waiting for transfers between devices, on_device(): lax.all_to_all(expert_out, 'expert', split_axis=0, concat_axis=0, tiled=T...  231 us
    all_to_all x1, waiting for transfers between devices, on_device(): lax.all_to_all(row_grad, 'expert', split_axis=0, concat_axis=0, tiled=True)  143 us
    gather x1, local copies, waits for them, and re-layouts, on_device(): returned_part.reshape(EXPERTS, CAP, MODEL_WIDTH)[flat_route, slot_index]  81.2 us
    gather x1, local copies, waits for them, and re-layouts, on_device(): row_back.reshape(EXPERTS, CAP, MODEL_WIDTH)[flat_route, slot_index]  80.9 us
    reduce_scatter x1, waiting for transfers between devices, on_device(): lax.psum_scatter(query_local.astype(jnp.bfloat16), 'fsdp', scatter_dimens...  38.5 us
    reduce_scatter x1, waiting for transfers between devices, on_device(): lax.psum_scatter(outproj_local.astype(jnp.bfloat16), 'fsdp', scatter_dime...  38.2 us
  transfers between devices with their start and end apart: 15, of which 12 were waited for; matrix products, arithmetic and copies ran while one was open for 27% of the time, Pallas kernels for 0%

commit v1 on v0

--- a/solution.py
+++ b/solution.py
@@ -60,6 +60,72 @@
     ) * HEAD_WIDTH ** (-0.5)
     causal = jnp.arange(length)[:, None] >= jnp.arange(length)[None, :]
     return jnp.where(causal, attention_scores, NEGATIVE)
+
+
+def dense_gates(rows, router_full, routes):
+    logits = jnp.dot(rows, router_full, preferred_element_type=jnp.float32)
+    named = jnp.any(routes[..., None] == jnp.arange(EXPERTS), axis=-2)
+    top = jnp.max(jnp.where(named, logits, -jnp.inf), axis=-1, keepdims=True)
+    powers = jnp.where(named, jnp.exp(jnp.where(named, logits - top, 0.0)), 0.0)
+    return powers / jnp.sum(powers, axis=-1, keepdims=True)
+
+
+def ring_gather(block, n_expert):
+    me = lax.axis_index("expert")
+    chips = n_expert // 2
+    chip, core = me // 2, me % 2
+    step_on = [(i, (i + 2) % n_expert) for i in range(n_expert)]
+    held = [block]
+    for _ in range(chips - 1):
+        held.append(lax.ppermute(held[-1], "expert", step_on))
+    swap = [(i, i ^ 1) for i in range(n_expert)]
+    gathered = jnp.zeros((chips, 2) + block.shape, block.dtype)
+    for k, part in enumerate(held):
+        other = lax.ppermute(part, "expert", swap)
+        source = (chip - k + chips) % chips
+        both = jnp.where(core == 0, jnp.stack([part, other]), jnp.stack([other, part]))
+        gathered = lax.dynamic_update_index_in_dim(gathered, both, source, 0)
+    return gathered.reshape((n_expert,) + block.shape)
+
+
+def butterfly_sum(block, bits):
+    size = lax.axis_size("fsdp")
+    me = lax.axis_index("fsdp")
+    width = block.shape[-1]
+    current = block.reshape(-1, width)
+    for bit in bits:
+        side = (me >> bit) & 1
+        halves = current.reshape(2, -1, width)
+        keep = lax.dynamic_index_in_dim(halves, side, 0, keepdims=False)
+        send = lax.dynamic_index_in_dim(halves, 1 - side, 0, keepdims=False)
+        got = lax.ppermute(send, "fsdp", [(i, i ^ (1 << bit)) for i in range(size)])
+        current = (keep.astype(jnp.float32) + got.astype(jnp.float32)).astype(jnp.bfloat16)
+    for bit in reversed(bits):
+        side = (me >> bit) & 1
+        got = lax.ppermute(current, "fsdp", [(i, i ^ (1 << bit)) for i in range(size)])
+        current = jnp.where(
+            side == 0, jnp.concatenate([current, got]), jnp.concatenate([got, current])
+        )
+    return current.reshape(block.shape)
+
+
+def fsdp_sum(block):
+    size = lax.axis_size("fsdp")
+    if size & (size - 1):
+        return lax.psum(block, "fsdp").astype(jnp.float32)
+    bits = list(range(size.bit_length() - 1))
+    half = block.shape[0] // 2
+    first = butterfly_sum(block[:half], bits)
+    second = butterfly_sum(block[half:], bits[::-1])
+    return jnp.concatenate([first, second]).astype(jnp.float32)
+
+
+def reduce_pack(parts, n_expert):
+    width = sum(part.shape[1] for part in parts)
+    pad = jnp.zeros((parts[0].shape[0], -width % 128), jnp.bfloat16)
+    packed = jnp.concatenate([part.astype(jnp.bfloat16) for part in parts] + [pad], axis=1)
+    packed = lax.psum_scatter(packed, "fsdp", scatter_dimension=0, tiled=True)
+    return lax.psum(packed, "expert").astype(jnp.float32)
 
 
 def on_device(
@@ -81,15 +147,32 @@
     token_rows = tokens.shape[0]
     exp_local = gate_weight.shape[0]
     query_group_width = QUERY_HEADS // KEY_VALUE_HEADS
-    attn_gain, query_full, key_full, value_full, outproj_full, moe_gain, router_full = (
-        lax.all_gather(norm_one, "fsdp", axis=0, tiled=True),
-        lax.all_gather(query_weight, "fsdp", axis=0, tiled=True),
-        lax.all_gather(key_projection_matrix, "fsdp", axis=0, tiled=True),
-        lax.all_gather(value_projection_matrix, "fsdp", axis=0, tiled=True),
-        lax.all_gather(out_weight, "fsdp", axis=0, tiled=True),
-        lax.all_gather(norm_two, "fsdp", axis=0, tiled=True),
-        lax.all_gather(router_weight, "fsdp", axis=0, tiled=True),
-    )
+    kv_width = KEY_VALUE_HEADS * HEAD_WIDTH
+    shard_rows = query_weight.shape[0]
+    first_pack = jnp.concatenate(
+        [
+            query_weight,
+            key_projection_matrix,
+            value_projection_matrix,
+            router_weight,
+            norm_one[:, None],
+            norm_two[:, None],
+            jnp.zeros((shard_rows, 128 - EXPERTS - 2), jnp.bfloat16),
+        ],
+        axis=1,
+    )
+    first_full = lax.all_gather(first_pack, "fsdp", axis=0, tiled=True)
+    qkv_width = MODEL_WIDTH + 2 * kv_width
+    query_full = first_full[:, :MODEL_WIDTH]
+    key_full = first_full[:, MODEL_WIDTH : MODEL_WIDTH + kv_width]
+    value_full = first_full[:, MODEL_WIDTH + kv_width : qkv_width]
+    qkv_full = first_full[:, :qkv_width]
+    router_full = first_full[:, qkv_width : qkv_width + EXPERTS]
+    attn_gain = first_full[:, qkv_width + EXPERTS]
+    moe_gain = first_full[:, qkv_width + EXPERTS + 1]
+    outproj_full = lax.all_gather(out_weight, "fsdp", axis=0, tiled=True)
+    grad_all = ring_gather(out_grad, n_expert)
+    routes_all = lax.all_gather(routes, "expert", axis=0, tiled=False)
     x_float = tokens.astype(jnp.float32)
     gain_first = attn_gain.astype(jnp.float32)
     normed_one, norm_one_back = jax.vjp(rms_scale, x_float, gain_first)
@@ -128,78 +211,64 @@
     gain_second = moe_gain.astype(jnp.float32)
     normed_two, norm_two_back = jax.vjp(rms_scale, resid_one, gain_second)
     moe_input = normed_two.astype(jnp.bfloat16)
-    logits = jnp.dot(moe_input, router_full, preferred_element_type=jnp.float32)
-    route_pick = (routes[:, :, None] == jnp.arange(EXPERTS)[None, None, :]).astype(jnp.float32)
-    chosen = jnp.sum(route_pick * logits[:, None, :], axis=-1)
-    chosen_top = jnp.max(chosen, axis=-1, keepdims=True)
-    chosen_exp = jnp.exp(chosen - chosen_top)
-    gates = chosen_exp / jnp.sum(chosen_exp, axis=-1, keepdims=True)
-    flat_route = routes.reshape(-1)
-    pick = (flat_route[:, None] == jnp.arange(EXPERTS)[None, :]).astype(jnp.int32)
-    running = jnp.cumsum(pick, axis=0) - 1
-    slot_index = jnp.sum(running * pick, axis=1)
-    send_rows = (
-        jnp.zeros((EXPERTS, CAP, MODEL_WIDTH), jnp.bfloat16)
-        .at[flat_route, slot_index]
-        .set(jnp.repeat(moe_input, TOPK, axis=0))
-    )
-    send_rows = send_rows.reshape(n_expert, exp_local, CAP, MODEL_WIDTH)
-    arrived_rows = lax.all_to_all(send_rows, "expert", split_axis=0, concat_axis=0, tiled=True)
+    moe_all = lax.all_gather(moe_input, "expert", axis=0, tiled=False)
+    gates = dense_gates(moe_input, router_full, routes)
+    first_expert = lax.axis_index("expert") * exp_local
+    own_ids = first_expert + jnp.arange(exp_local)
+    own_mask = jnp.any(routes_all[:, :, :, None] == own_ids, axis=2)
+    earlier = (jnp.arange(token_rows)[:, None] > jnp.arange(token_rows)[None, :]).astype(
+        jnp.bfloat16
+    )
+    slots = jnp.einsum(
+        "tu,nue->net", earlier, own_mask.astype(jnp.bfloat16), preferred_element_type=jnp.float32
+    )
+    slots = jnp.where(jnp.swapaxes(own_mask, 1, 2), slots, -1.0).astype(jnp.int32)
+    hit = slots[:, :, None, :] == jnp.arange(CAP)[None, None, :, None]
+    place = hit.astype(jnp.bfloat16)
+    grad_rows = jnp.einsum(
+        "nest,ntd->nesd", place, grad_all, preferred_element_type=jnp.float32
+    ).astype(jnp.bfloat16)
+    gates_all = dense_gates(moe_all, router_full, routes_all)
+    gates_own = lax.dynamic_slice_in_dim(gates_all, first_expert, exp_local, axis=2)
+    gate_slot = jnp.sum(
+        jnp.where(hit, jnp.swapaxes(gates_own, 1, 2)[:, :, None, :], 0.0), axis=-1, keepdims=True
+    )
+    arrived_rows = jnp.einsum(
+        "nest,ntd->nesd", place, moe_all, preferred_element_type=jnp.float32
+    ).astype(jnp.bfloat16)
     gate_part = jnp.einsum(
         "nesd,edf->nesf", arrived_rows, gate_weight, preferred_element_type=jnp.float32
     )
     up_part = jnp.einsum(
         "nesd,edf->nesf", arrived_rows, up_weight, preferred_element_type=jnp.float32
     )
-    hidden_part = (gate_part * jax.nn.sigmoid(gate_part) * up_part).astype(jnp.bfloat16)
-    expert_out = jnp.einsum(
-        "nesf,efd->nesd", hidden_part, down_weight, preferred_element_type=jnp.float32
-    ).astype(jnp.bfloat16)
-    returned_part = lax.all_to_all(expert_out, "expert", split_axis=0, concat_axis=0, tiled=True)
-    back_rows = (
-        returned_part.reshape(EXPERTS, CAP, MODEL_WIDTH)[flat_route, slot_index]
-        .astype(jnp.float32)
-        .reshape(token_rows, TOPK, MODEL_WIDTH)
-    )
-    moe_sum = jnp.sum(gates[:, :, None] * back_rows, axis=1)
-    block_out = (resid_one + moe_sum).astype(jnp.bfloat16)
-    grad_float = out_grad.astype(jnp.float32)
-    gate_score = jnp.sum(back_rows * grad_float[:, None, :], axis=-1)
-    chosen_grad = gates * (gate_score - jnp.sum(gates * gate_score, axis=-1, keepdims=True))
-    logit_grad = jnp.sum(chosen_grad[:, :, None] * route_pick, axis=1)
-    router_local = jnp.dot(moe_input.astype(jnp.float32).T, logit_grad, precision=HIGH_PRECISION)
-    router_back = jnp.dot(logit_grad, router_full.astype(jnp.float32).T, precision=HIGH_PRECISION)
-    slot_grad = (
-        (gates[:, :, None] * grad_float[:, None, :])
-        .astype(jnp.bfloat16)
-        .reshape(token_rows * TOPK, MODEL_WIDTH)
-    )
-    grad_send = (
-        jnp.zeros((EXPERTS, CAP, MODEL_WIDTH), jnp.bfloat16)
-        .at[flat_route, slot_index]
-        .set(slot_grad)
-    )
-    grad_send = grad_send.reshape(n_expert, exp_local, CAP, MODEL_WIDTH)
-    grad_arrived = lax.all_to_all(grad_send, "expert", split_axis=0, concat_axis=0, tiled=True)
     sigma = jax.nn.sigmoid(gate_part)
     silu_value = gate_part * sigma
-    hidden = (silu_value * up_part).astype(jnp.bfloat16)
+    hidden = silu_value * up_part
+    hidden_scaled = (gate_slot * hidden).astype(jnp.bfloat16)
+    expert_out = jnp.einsum(
+        "nesf,efd->nesd", hidden_scaled, down_weight, preferred_element_type=jnp.float32
+    ).astype(jnp.bfloat16)
+    out_home = jnp.einsum(
+        "nest,nesd->ntd", place, expert_out, preferred_element_type=jnp.float32
+    ).astype(jnp.bfloat16)
+    out_home, grad_rows = lax.optimization_barrier((out_home, grad_rows))
+    moe_sum = lax.psum_scatter(out_home, "expert", scatter_dimension=0, tiled=False)
     down_local = jnp.einsum(
-        "nesf,nesd->efd", hidden, grad_arrived, preferred_element_type=jnp.float32
-    )
-    hidden_grad = jnp.einsum(
-        "nesd,efd->nesf", grad_arrived, down_weight, preferred_element_type=jnp.float32
-    )
+        "nesf,nesd->efd", hidden_scaled, grad_rows, preferred_element_type=jnp.float32
+    )
+    hidden_back = jnp.einsum(
+        "nesd,efd->nesf", grad_rows, down_weight, preferred_element_type=jnp.float32
+    )
+    score_slot = jnp.sum(hidden * hidden_back, axis=-1)
+    score_token = jnp.sum(jnp.where(hit, score_slot[:, :, :, None], 0.0), axis=2)
+    gate_score = lax.all_to_all(score_token, "expert", split_axis=0, concat_axis=0, tiled=True)
+    gate_score = gate_score.reshape(EXPERTS, token_rows).T
+    hidden_grad = gate_slot * hidden_back
     gate_low = (hidden_grad * up_part * sigma * (1.0 + gate_part * (1.0 - sigma))).astype(
         jnp.bfloat16
     )
     up_low = (hidden_grad * silu_value).astype(jnp.bfloat16)
-    gate_local = jnp.einsum(
-        "nesd,nesf->edf", arrived_rows, gate_low, preferred_element_type=jnp.float32
-    )
-    up_local = jnp.einsum(
-        "nesd,nesf->edf", arrived_rows, up_low, preferred_element_type=jnp.float32
-    )
     row_grad = jnp.einsum(
         "nesf,edf->nesd", gate_low, gate_weight, preferred_element_type=jnp.float32
     )
@@ -207,22 +276,36 @@
         row_grad
         + jnp.einsum("nesf,edf->nesd", up_low, up_weight, preferred_element_type=jnp.float32)
     ).astype(jnp.bfloat16)
-    row_back = lax.all_to_all(row_grad, "expert", split_axis=0, concat_axis=0, tiled=True)
-    gate_sum, up_sum, down_sum = (
-        lax.psum(gate_local.astype(jnp.bfloat16), "fsdp").astype(jnp.float32),
-        lax.psum(up_local.astype(jnp.bfloat16), "fsdp").astype(jnp.float32),
-        lax.psum(down_local.astype(jnp.bfloat16), "fsdp").astype(jnp.float32),
-    )
-    home_rows = (
-        row_back.reshape(EXPERTS, CAP, MODEL_WIDTH)[flat_route, slot_index]
-        .astype(jnp.float32)
-        .reshape(token_rows, TOPK, MODEL_WIDTH)
-    )
-    normed_two_grad = jnp.sum(home_rows, axis=1) + router_back
+    row_home = jnp.einsum(
+        "nest,nesd->ntd", place, row_grad, preferred_element_type=jnp.float32
+    ).astype(jnp.bfloat16)
+    row_sum = lax.psum_scatter(row_home, "expert", scatter_dimension=0, tiled=False)
+    block_out = (resid_one + moe_sum.astype(jnp.float32)).astype(jnp.bfloat16)
+    gate_local = jnp.einsum(
+        "nesd,nesf->edf", arrived_rows, gate_low, preferred_element_type=jnp.float32
+    )
+    up_local = jnp.einsum(
+        "nesd,nesf->edf", arrived_rows, up_low, preferred_element_type=jnp.float32
+    )
+    down_low = down_local.astype(jnp.bfloat16)
+    gate_grad_low = gate_local.astype(jnp.bfloat16)
+    up_grad_low = up_local.astype(jnp.bfloat16)
+    down_sum = fsdp_sum(down_low)
+    gate_sum = fsdp_sum(gate_grad_low)
+    up_sum = fsdp_sum(up_grad_low)
+    row_sum, _, _, _ = lax.optimization_barrier(
+        (row_sum, down_low, gate_grad_low, up_grad_low)
+    )
+    grad_float = out_grad.astype(jnp.float32)
+    logit_grad = gates * (gate_score - jnp.sum(gates * gate_score, axis=-1, keepdims=True))
+    router_local = jnp.dot(moe_input.astype(jnp.float32).T, logit_grad, precision=HIGH_PRECISION)
+    router_back = jnp.dot(logit_grad, router_full.astype(jnp.float32).T, precision=HIGH_PRECISION)
+    normed_two_grad = row_sum.astype(jnp.float32) + router_back
     resid_from_norm, gain_two_grad = norm_two_back(normed_two_grad)
     resid_grad = grad_float + resid_from_norm
     proj_low = resid_grad.astype(jnp.bfloat16)
     outproj_local = inner_rows(attn_low, proj_low)
+    early = reduce_pack([outproj_local, router_local, gain_two_grad[:, None]], n_expert)
     head_outputs_gradient = (
         outer_cols(proj_low, outproj_full)
         .astype(jnp.bfloat16)
@@ -277,38 +360,16 @@
     )
     x_from_norm, gain_one_grad = norm_one_back(normed_one_grad)
     input_grad = resid_grad + x_from_norm
-    gain_a, query_a, key_a, value_a, outproj_a, gain_b, router_a = (
-        lax.psum_scatter(
-            gain_one_grad.astype(jnp.bfloat16), "fsdp", scatter_dimension=0, tiled=True
-        ).astype(jnp.float32),
-        lax.psum_scatter(
-            query_local.astype(jnp.bfloat16), "fsdp", scatter_dimension=0, tiled=True
-        ).astype(jnp.float32),
-        lax.psum_scatter(
-            key_local.astype(jnp.bfloat16), "fsdp", scatter_dimension=0, tiled=True
-        ).astype(jnp.float32),
-        lax.psum_scatter(
-            value_local.astype(jnp.bfloat16), "fsdp", scatter_dimension=0, tiled=True
-        ).astype(jnp.float32),
-        lax.psum_scatter(
-            outproj_local.astype(jnp.bfloat16), "fsdp", scatter_dimension=0, tiled=True
-        ).astype(jnp.float32),
-        lax.psum_scatter(
-            gain_two_grad.astype(jnp.bfloat16), "fsdp", scatter_dimension=0, tiled=True
-        ).astype(jnp.float32),
-        lax.psum_scatter(
-            router_local.astype(jnp.bfloat16), "fsdp", scatter_dimension=0, tiled=True
-        ).astype(jnp.float32),
-    )
-    gain_c, query_c, key_c, value_c, outproj_c, gain_d, router_c = (
-        lax.psum(gain_a.astype(jnp.bfloat16), "expert").astype(jnp.float32),
-        lax.psum(query_a.astype(jnp.bfloat16), "expert").astype(jnp.float32),
-        lax.psum(key_a.astype(jnp.bfloat16), "expert").astype(jnp.float32),
-        lax.psum(value_a.astype(jnp.bfloat16), "expert").astype(jnp.float32),
-        lax.psum(outproj_a.astype(jnp.bfloat16), "expert").astype(jnp.float32),
-        lax.psum(gain_b.astype(jnp.bfloat16), "expert").astype(jnp.float32),
-        lax.psum(router_a.astype(jnp.bfloat16), "expert").astype(jnp.float32),
-    )
+    late = reduce_pack(
+        [query_local, key_local, value_local, gain_one_grad[:, None]], n_expert
+    )
+    query_c = late[:, :MODEL_WIDTH]
+    key_c = late[:, MODEL_WIDTH : MODEL_WIDTH + kv_width]
+    value_c = late[:, MODEL_WIDTH + kv_width : qkv_width]
+    gain_c = late[:, qkv_width]
+    outproj_c = early[:, :MODEL_WIDTH]
+    router_c = early[:, MODEL_WIDTH : MODEL_WIDTH + EXPERTS]
+    gain_d = early[:, MODEL_WIDTH + EXPERTS]
     return (
         block_out,
         input_grad,

time: 1710 us -> 1050 us (0.61)
  waiting for transfers between devices: 1050 us -> 536 us
  local copies, waits for them, and re-layouts: 217 us -> 64 us
  matrix products: 211 us -> 254 us
  other arithmetic: 119 us -> 77.5 us
  starting transfers between devices: 23 us -> 58.6 us
  blocking collectives: 63.8 us -> 33 us
    all_to_all x4 -> x1, waiting for transfers between devices: 855 us -> 0.01 us  [on_device(): lax.all_to_all(score_token, 'expert', split_axis=0, concat_axis=0, tiled=...]
    ppermute x0 -> x31, waiting for transfers between devices: none -> 291 us  [the longest x12 121 us: butterfly_sum(): got = lax.ppermute(send, 'fsdp', [(i, i ^ 1 << bit) for i in range(size)])]
    gather x2 -> x0, local copies, waits for them, and re-layouts: 162 us -> none  [the longest x1 81.2 us: on_device(): returned_part.reshape(EXPERTS, CAP, MODEL_WIDTH)[flat_route, slot_index]]
    ppermute x0 -> x31, starting transfers between devices: none -> 54.7 us  [the longest x3 27.1 us: ring_gather(): held.append(lax.ppermute(held[-1], 'expert', step_on))]
    concatenate x0 -> x3, local copies, waits for them, and re-layouts: none -> 38.6 us  [the longest x2 32.4 us: reduce_pack(): jnp.concatenate([part.astype(jnp.bfloat16) for part in parts] + [pad], ax...]
    reduce_scatter x5 -> x4, waiting for transfers between devices: 87.2 us -> 125 us  [the longest x1 86.6 us: on_device(): lax.psum_scatter(out_home, 'expert', scatter_dimension=0, tiled=False)]
    dot_general x5 -> x9, matrix products: 67 us -> 103 us  [the longest x1 22.5 us: on_device(): jnp.einsum('nesd,efd->nesf', grad_rows, down_weight, preferred_element_ty...]
    psum x1 -> x0, blocking collectives: 28.6 us -> none  [on_device(): lax.psum(gain_a.astype(jnp.bfloat16), 'expert').astype(jnp.float32)]
  transfers between devices with their start and end apart: 15 -> 40, of which waited for: 12 -> 18; matrix products, arithmetic and copies ran while one was open for 27% -> 21% of each run, Pallas kernels for 0% -> 0%
where the time goes in v1:
time: 1050 us; the launch traced here: 1040 us
  waiting for transfers between devices  536 us (51%)
  matrix products  254 us (24%)
  other arithmetic  77.5 us (7%)
  local copies, waits for them, and re-layouts  64 us (6%)
  starting transfers between devices  58.6 us (6%)
  blocking collectives  33 us (3%)
  between operations  16 us (2%)
    ppermute x12, waiting for transfers between devices, butterfly_sum(): got = lax.ppermute(send, 'fsdp', [(i, i ^ 1 << bit) for i in range(size)])  121 us
    ppermute x3, waiting for transfers between devices, ring_gather(): held.append(lax.ppermute(held[-1], 'expert', step_on))  88.6 us
    reduce_scatter x1, waiting for transfers between devices, on_device(): lax.psum_scatter(out_home, 'expert', scatter_dimension=0, tiled=False)  86.6 us
    ppermute x12, waiting for transfers between devices, butterfly_sum(): lax.ppermute(current, 'fsdp', [(i, i ^ 1 << bit) for i in range(size)])  81.9 us
    psum x1, waiting for transfers between devices, reduce_pack(): return lax.psum(packed, 'expert').astype(jnp.float32)  56.6 us
    all_gather x1, waiting for transfers between devices, on_device(): first_full = lax.all_gather(first_pack, 'fsdp', axis=0, tiled=True)  54.9 us
    reduce_scatter x1, waiting for transfers between devices, on_device(): lax.psum_scatter(row_home, 'expert', scatter_dimension=0, tiled=False)  38.1 us
    all_gather x1, blocking collectives, on_device(): routes_all = lax.all_gather(routes, 'expert', axis=0, tiled=False)  33 us
  transfers between devices with their start and end apart: 40, of which 18 were waited for; matrix products, arithmetic and copies ran while one was open for 21% of the time, Pallas kernels for 0%

profile of v1, /device:TPU:0, one launch (start us, length us, event | category | flops | bytes accessed | tf_op | source)
XLA Modules:
  0.0 1038.9 jit_solution(13058409088596116917)
XLA Ops:
  21.1 54.9 %all-gather.6.cloned.1.call-done = bf16[1024,2176]{0,1:T(8,128)(2,1)} async-done(((bf16[256,2176]{0,1:T(8,128)(2,1)}), bf16[1024,2176]{0,1:T(8,128)(2,1)}) %all-gather.6.cloned.1.call-update) | async-done | bytes 4456464 | tf_op jit(solution)/shard_map/all_gather | solution.py:164
  120.3 40.3 %collective-permute-done.1 = bf16[512,1024]{1,0:T(8,128)(2,1)} collective-permute-done((bf16[512,1024]{1,0:T(8,128)(2,1)S(1)}, bf16[512,1024]{1,0:T(8,128)(2,1)}, u32[]{:S(2)}, u32[]{:S(2)}) %collective-permute-start.1) | collective-permute-done | bytes 1048608 | tf_op jit(solution)/shard_map/ppermute | solution.py:80
  160.6 14.7 %collective-permute-start.3 = (bf16[512,1024]{1,0:T(8,128)(2,1)}, bf16[512,1024]{1,0:T(8,128)(2,1)}, u32[]{:S(2)}, u32[]{:S(2)}) collective-permute-start(bf16[512,1024]{1,0:T(8,128)(2,1)} %collective-permute-done.1), channel_id=1, source_target_pairs={{0,8},{4,12},{8,16},{12,20},{16,24},{20,28},{24,0},{28,4},{1,9},{5... | collective-permute-start | bytes 3145736 | tf_op jit(solution)/shard_map/ppermute | solution.py:80
  175.3 48.2 %collective-permute-done.3 = bf16[512,1024]{1,0:T(8,128)(2,1)} collective-permute-done((bf16[512,1024]{1,0:T(8,128)(2,1)}, bf16[512,1024]{1,0:T(8,128)(2,1)}, u32[]{:S(2)}, u32[]{:S(2)}) %collective-permute-start.3) | collective-permute-done | bytes 1048608 | tf_op jit(solution)/shard_map/ppermute | solution.py:80
  234.9 33.0 %all-gather = s32[4096,8]{0,1:T(8,128)S(1)} all-gather(s32[512,8]{0,1:T(8,128)S(1)} %copy-done.41), channel_id=2, replica_groups=mesh['expert'=8,'fsdp'=4] {'expert'}, dimensions={0}, use_global_device_ids=true | all-gather | bytes 147456 | tf_op jit(solution)/shard_map/all_gather | solution.py:175
  324.1 17.7 %multiply_convert_fusion.1 = (bf16[8,4,192,512]{3,2,0,1:T(8,128)(2,1)}, f32[4,8,192,512]{3,2,1,0:T(8,128)}) fusion(f32[8,4,192]{2,0,1:T(8,128)S(1)} %copy.114, f32[4,8,192,512]{3,2,1,0:T(8,128)} %fusion.28, bf16[4,1024,512]{2,1,0:T(8,128)(2,1)} %param.22, bf16[8,4,192,1024]{3,2,1,0:T(8,128)(2,1)} %fusion.34), kind=kOutput, calls=%fused_computation.37 | convolution fusion | flops 6464471040 | bytes 48259072 | tf_op jit(solution)/shard_map/nesd,edf->nesf/dot_general | solution.py:242
  341.8 18.7 %bitcast_convert_fusion.1 = bf16[8,512,1024]{2,1,0:T(8,128)(2,1)} fusion(s32[8,4,512]{2,1,0:T(4,128)S(1)} %copy.113, bf16[8,4,192,512]{3,2,0,1:T(8,128)(2,1)} %get-tuple-element.104, bf16[4,512,1024]{2,1,0:T(8,128)(2,1)} %param.23), kind=kOutput, calls=%fused_computation.8 | convolution fusion | flops 12898533376 | bytes 18939904 | tf_op jit(solution)/shard_map/nest,nesd->ntd/dot_general | solution.py:252
  360.5 22.5 %fusion.9 = (f32[8,4,192]{2,0,1:T(8,128)S(1)}, bf16[8,4,192,512]{3,2,0,1:T(8,128)(2,1)}, bf16[8,4,192,512]{3,2,0,1:T(8,128)(2,1)}) fusion(f32[4,8,192,512]{3,2,1,0:T(8,128)} %get-tuple-element.105, f32[4,8,192,512]{3,2,1,0:T(8,128)} %fusion.28, f32[8,4,192]{2,0,1:T(8,128)S(1)} %copy.114, bf16[4,512,1024]{2,1,0:T(8,128)(2,1)} %param.23, ...), kind=kOutput, calls=%fused_computation.19 | convolution fusion | flops 6495922176 | bytes 54575104 | tf_op jit(solution)/shard_map/nesd,efd->nesf/dot_general | solution.py:260
  382.9 14.9 %fusion.54 = f32[4,8,192,1024]{3,2,0,1:T(8,128)} fusion(bf16[8,4,192,512]{3,2,0,1:T(8,128)(2,1)} %get-tuple-element.73, bf16[4,1024,512]{2,1,0:T(8,128)(2,1)S(1)} %copy-done.56), kind=kOutput, calls=%fused_computation.70 | convolution fusion | flops 6442450944 | bytes 35651584 | tf_op jit(solution)/shard_map/nesf,edf->nesd/dot_general | solution.py:272
  397.8 22.2 %bitcast_convert_fusion = bf16[8,512,1024]{2,1,0:T(8,128)(2,1)} fusion(f32[4,8,192,1024]{3,2,0,1:T(8,128)} %fusion.54, s32[8,4,512]{2,1,0:T(4,128)S(1)} %copy.113, bf16[8,4,192,512]{3,2,0,1:T(8,128)(2,1)} %get-tuple-element.74, bf16[4,1024,512]{2,1,0:T(8,128)(2,1)} %param.22), kind=kOutput, calls=%fused_computation.7 | convolution fusion | flops 12904824832 | bytes 44105728 | tf_op jit(solution)/shard_map/nest,nesd->ntd/dot_general | solution.py:279
  430.4 13.6 %bitcast_convert_fusion.3 = bf16[4,1024,512]{2,1,0:T(8,128)(2,1)} fusion(bf16[8,4,192,1024]{3,2,1,0:T(8,128)(2,1)} %fusion.34, bf16[8,4,192,512]{3,2,0,1:T(8,128)(2,1)} %get-tuple-element.73), kind=kOutput, calls=%fused_computation.52 | convolution fusion | flops 6444548096 | bytes 23068672 | tf_op jit(solution)/shard_map/nesd,nesf->edf/dot_general | solution.py:284
  471.1 38.1 %reduce-scatter.7.cloned.1.call-done = bf16[1,512,1024]{2,1,0:T(8,128)(2,1)} async-done(((bf16[8,512,1024]{2,1,0:T(8,128)(2,1)}), bf16[1,512,1024]{2,1,0:T(8,128)(2,1)}) %reduce-scatter.7.cloned.1.call-update) | async-done | bytes 1048592 | tf_op jit(solution)/shard_map/reduce_scatter | solution.py:282
  513.3 86.6 %reduce-scatter.5.cloned.1.call-done = bf16[1,512,1024]{2,1,0:T(8,128)(2,1)} async-done(((bf16[8,512,1024]{2,1,0:T(8,128)(2,1)}), bf16[1,512,1024]{2,1,0:T(8,128)(2,1)}) %reduce-scatter.5.cloned.1.call-update) | async-done | bytes 1048592 | tf_op jit(solution)/shard_map/reduce_scatter | solution.py:256
  620.3 15.7 %fusion.1 = (f32[8,2,512]{2,1,0:T(2,128)S(1)}, f32[8,512,512,2]{2,1,3,0:T(8,128)}) fusion(f32[8,2,512,512]{2,3,1,0:T(8,128)} %get-tuple-element.99, f32[8,2,512]{2,1,0:T(2,128)S(1)} %bitcast.349, bf16[512,8,64,1]{0,2,3,1:T(8,128)(2,1)S(1)} %bitcast.348, bf16[512,8,2,64]{0,3,2,1:T(8,128)(2,1)S(1)} %bitcast.304), kind=kOutput, calls=%fused_computation.4 | convolution fusion | flops 549445632 | bytes 35192832 | tf_op jit(solution)/shard_map/mhwo,pho->hwmp/dot_general | solution.py:325
  680.2 20.2 %concatenate.174 = bf16[1024,2176]{0,1:T(8,128)(2,1)} concatenate(bf16[1024,1024]{0,1:T(8,128)(2,1)} %convolution_convert_fusion, bf16[1024,512]{0,1:T(8,128)(2,1)} %convolution_convert_fusion.4, bf16[1024,512]{0,1:T(8,128)(2,1)S(1)} %copy-done.32, bf16[1024,1]{0,1:T(2,128)(2,1)S(1)} %convert_element_type.464, bf16[1024,127]{0,1:T(8,128)(2,1)S(1)} %broadcast_in_dim.138), dimensions={1} | concatenate | bytes 8912896 | tf_op jit(solution)/shard_map/concatenate | solution.py:126
  710.5 41.1 %collective-permute-done.19 = bf16[1024,512]{1,0:T(8,128)(2,1)S(1)} collective-permute-done((bf16[1024,512]{1,0:T(8,128)(2,1)S(1)}, bf16[1024,512]{1,0:T(8,128)(2,1)S(1)}, u32[]{:S(2)}, u32[]{:S(2)}) %collective-permute-start.19) | collective-permute-done | bytes 1048608 | tf_op jit(solution)/shard_map/ppermute | solution.py:101
  755.6 31.9 %collective-permute-done.11 = bf16[1024,512]{1,0:T(8,128)(2,1)S(1)} collective-permute-done((bf16[1024,512]{1,0:T(8,128)(2,1)S(1)}, bf16[1024,512]{1,0:T(8,128)(2,1)S(1)}, u32[]{:S(2)}, u32[]{:S(2)}) %collective-permute-start.11) | collective-permute-done | bytes 1048608 | tf_op jit(solution)/shard_map/ppermute | solution.py:101
  789.3 21.2 %collective-permute-done.27 = bf16[512,1024]{1,0:T(8,128)(2,1)S(1)} collective-permute-done((bf16[512,1024]{1,0:T(8,128)(2,1)S(1)}, bf16[512,1024]{1,0:T(8,128)(2,1)S(1)}, u32[]{:S(2)}, u32[]{:S(2)}) %collective-permute-start.27) | collective-permute-done | bytes 1048608 | tf_op jit(solution)/shard_map/ppermute | solution.py:101
  823.9 18.8 %collective-permute-done.28 = bf16[256,1024]{1,0:T(8,128)(2,1)S(1)} collective-permute-done((bf16[256,1024]{1,0:T(8,128)(2,1)S(1)}, bf16[256,1024]{1,0:T(8,128)(2,1)S(1)}, u32[]{:S(2)}, u32[]{:S(2)}) %collective-permute-start.28) | collective-permute-done | bytes 524320 | tf_op jit(solution)/shard_map/ppermute | solution.py:101
  847.7 18.3 %collective-permute-done.29 = bf16[256,1024]{1,0:T(8,128)(2,1)S(1)} collective-permute-done((bf16[256,1024]{1,0:T(8,128)(2,1)S(1)}, bf16[256,1024]{1,0:T(8,128)(2,1)S(1)}, u32[]{:S(2)}, u32[]{:S(2)}) %collective-permute-start.29) | collective-permute-done | bytes 524320 | tf_op jit(solution)/shard_map/ppermute | solution.py:105
  883.0 22.6 %collective-permute-done.9 = bf16[512,512]{1,0:T(8,128)(2,1)S(1)} collective-permute-done((bf16[512,512]{1,0:T(8,128)(2,1)S(1)}, bf16[512,512]{1,0:T(8,128)(2,1)S(1)}, u32[]{:S(2)}, u32[]{:S(2)}) %collective-permute-start.9) | collective-permute-done | bytes 524320 | tf_op jit(solution)/shard_map/ppermute | solution.py:105
  911.8 16.2 %collective-permute-done.22 = bf16[1024,512]{1,0:T(8,128)(2,1)S(1)} collective-permute-done((bf16[1024,512]{1,0:T(8,128)(2,1)S(1)}, bf16[1024,512]{1,0:T(8,128)(2,1)S(1)}, u32[]{:S(2)}, u32[]{:S(2)}) %collective-permute-start.22) | collective-permute-done | bytes 1048608 | tf_op jit(solution)/shard_map/ppermute | solution.py:105
  929.5 17.2 %collective-permute-done.14 = bf16[1024,512]{1,0:T(8,128)(2,1)S(1)} collective-permute-done((bf16[1024,512]{1,0:T(8,128)(2,1)S(1)}, bf16[1024,512]{1,0:T(8,128)(2,1)S(1)}, u32[]{:S(2)}, u32[]{:S(2)}) %collective-permute-start.14) | collective-permute-done | bytes 1048608 | tf_op jit(solution)/shard_map/ppermute | solution.py:105
  964.2 56.6 %all-reduce.3.cloned.1.call-done = (bf16[256,2176]{0,1:T(8,128)(2,1)}, bf16[256,1152]{0,1:T(8,128)(2,1)}) async-done(((bf16[256,2176]{0,1:T(8,128)(2,1)}, bf16[256,1152]{0,1:T(8,128)(2,1)}), (bf16[256,2176]{0,1:T(8,128)(2,1)}, bf16[256,1152]{0,1:T(8,128)(2,1)})) %all-reduce.3.cloned.1.call-update) | async-done | bytes 1703952 | tf_op jit(solution)/shard_map/psum | solution.py:128
  (339 shorter events, 318.1 us)
Async XLA Ops:
  7.2 68.7 %all-gather.6.cloned.1.call-start = ((), (), s32[]{:S(2)}) async-start(), calls=%async_computation.5 | async-start | bytes 5570560 | tf_op jit(solution)/shard_map/all_gather | solution.py:164
  18.3 94.8 %all-gather.8.cloned.1.call-start = ((), (), s32[]{:S(2)}) async-start(), calls=%async_computation.6 | async-start | bytes 2621440 | tf_op jit(solution)/shard_map/all_gather | solution.py:173
  19.1 273.8 %all-gather.10.cloned.1.call-start = ((), (), s32[]{:S(2)}) async-start(), calls=%async_computation.11 | async-start | bytes 9437184 | tf_op jit(solution)/shard_map/all_gather | solution.py:214
  118.7 390.4 %reduce-scatter.7.cloned.1.call-start = ((), (), s32[]{:S(2)}) async-start(), calls=%async_computation.8 | async-start | bytes 9437184 | tf_op jit(solution)/shard_map/reduce_scatter | solution.py:282
  118.8 41.8 %collective-permute-start.1 = (bf16[512,1024]{1,0:T(8,128)(2,1)S(1)}, bf16[512,1024]{1,0:T(8,128)(2,1)}, u32[]{:S(2)}, u32[]{:S(2)}) collective-permute-start(bf16[512,1024]{1,0:T(8,128)(2,1)S(1)} %copy-done.14), channel_id=1, source_target_pairs={{0,8},{4,12},{8,16},{12,20},{16,24},{20,28},{24,0},{28,4},{1,9},{5... | collective-permute-start | bytes 3145736 | tf_op jit(solution)/shard_map/ppermute | solution.py:80
  160.6 62.9 %collective-permute-start.3 = (bf16[512,1024]{1,0:T(8,128)(2,1)}, bf16[512,1024]{1,0:T(8,128)(2,1)}, u32[]{:S(2)}, u32[]{:S(2)}) collective-permute-start(bf16[512,1024]{1,0:T(8,128)(2,1)} %collective-permute-done.1), channel_id=1, source_target_pairs={{0,8},{4,12},{8,16},{12,20},{16,24},{20,28},{24,0},{28,4},{1,9},{5... | collective-permute-start | bytes 3145736 | tf_op jit(solution)/shard_map/ppermute | solution.py:80
  223.6 44.6 %collective-permute-start.5 = (bf16[512,1024]{1,0:T(8,128)(2,1)}, bf16[512,1024]{1,0:T(8,128)(2,1)S(1)}, u32[]{:S(2)}, u32[]{:S(2)}) collective-permute-start(bf16[512,1024]{1,0:T(8,128)(2,1)} %collective-permute-done.3), channel_id=1, source_target_pairs={{0,8},{4,12},{8,16},{12,20},{16,24},{20,28},{24,0},{28,4},{1,9},{5... | collective-permute-start | bytes 3145736 | tf_op jit(solution)/shard_map/ppermute | solution.py:80
  234.9 42.0 %collective-permute-start.4 = (bf16[512,1024]{1,0:T(8,128)(2,1)}, bf16[512,1024]{1,0:T(8,128)(2,1)}, u32[]{:S(2)}, u32[]{:S(2)}) collective-permute-start(bf16[512,1024]{1,0:T(8,128)(2,1)} %collective-permute-done.3), channel_id=1, source_target_pairs={{0,4},{4,0},{8,12},{12,8},{16,20},{20,16},{24,28},{28,24},{1,5},{5... | collective-permute-start | bytes 3145736 | tf_op jit(solution)/shard_map/ppermute | solution.py:84
  420.1 179.8 %reduce-scatter.5.cloned.1.call-start = ((), (), s32[]{:S(2)}) async-start(), calls=%async_computation.7 | async-start | bytes 9437184 | tf_op jit(solution)/shard_map/reduce_scatter | solution.py:256
  427.0 43.4 %all-to-all-start = ((f32[8,4,512]{2,1,0:T(4,128)}), f32[8,4,512]{2,1,0:T(4,128)S(1)}, u32[]{:S(2)}, u32[]{:S(2)}) async-start(f32[8,4,512]{2,1,0:T(4,128)} %select_reduce_fusion), calls=%async_computation.2 | async-start | bytes 131072 | tf_op jit(solution)/shard_map/all_to_all | solution.py:265
  430.4 525.5 %reduce-scatter.11.cloned.1.call-start = ((), (), s32[]{:S(2)}) async-start(), calls=%async_computation.10 | async-start | bytes 2949120 | tf_op jit(solution)/shard_map/reduce_scatter | solution.py:127
  620.2 335.7 %reduce-scatter.9.cloned.1.call-start = ((), (), s32[]{:S(2)}) async-start(), calls=%async_computation.9 | async-start | bytes 5570560 | tf_op jit(solution)/shard_map/reduce_scatter | solution.py:127
  700.5 320.2 %all-reduce.3.cloned.1.call-start = ((), (), s32[]{:S(2)}) async-start(), calls=%async_computation.12 | async-start | bytes 3407872 | tf_op jit(solution)/shard_map/psum | solution.py:128
  703.5 48.1 %collective-permute-start.19 = (bf16[1024,512]{1,0:T(8,128)(2,1)S(1)}, bf16[1024,512]{1,0:T(8,128)(2,1)S(1)}, u32[]{:S(2)}, u32[]{:S(2)}) collective-permute-start(bf16[1024,512]{1,0:T(8,128)(2,1)S(1)} %dynamic-slice_bitcast_fusion.2), channel_id=1, source_target_pairs={{0,2},{1,3},{2,0},{3,1},{4,6},{5,7},{6,4},{7,5},{8,10},{9,11},{10,... | collective-permute-start | bytes 3145736 | tf_op jit(solution)/shard_map/ppermute | solution.py:101
  705.4 48.2 %collective-permute-start.15 = (bf16[1024,512]{1,0:T(8,128)(2,1)S(1)}, bf16[1024,512]{1,0:T(8,128)(2,1)S(1)}, u32[]{:S(2)}, u32[]{:S(2)}) collective-permute-start(bf16[1024,512]{1,0:T(8,128)(2,1)S(1)} %dynamic-slice_bitcast_fusion.3), channel_id=1, source_target_pairs={{0,1},{1,0},{2,3},{3,2},{4,5},{5,4},{6,7},{7,6},{8,9},{9,8},{10,11... | collective-permute-start | bytes 3145736 | tf_op jit(solution)/shard_map/ppermute | solution.py:101
  707.1 80.4 %collective-permute-start.11 = (bf16[1024,512]{1,0:T(8,128)(2,1)S(1)}, bf16[1024,512]{1,0:T(8,128)(2,1)S(1)}, u32[]{:S(2)}, u32[]{:S(2)}) collective-permute-start(bf16[1024,512]{1,0:T(8,128)(2,1)S(1)} %dynamic-slice_bitcast_fusion.4), channel_id=1, source_target_pairs={{0,2},{1,3},{2,0},{3,1},{4,6},{5,7},{6,4},{7,5},{8,10},{9,11},{10,... | collective-permute-start | bytes 3145736 | tf_op jit(solution)/shard_map/ppermute | solution.py:101
  707.8 105.7 %collective-permute-start.7 = (bf16[1024,512]{1,0:T(8,128)(2,1)S(1)}, bf16[1024,512]{1,0:T(8,128)(2,1)S(1)}, u32[]{:S(2)}, u32[]{:S(2)}) collective-permute-start(bf16[1024,512]{1,0:T(8,128)(2,1)S(1)} %dynamic-slice_bitcast_fusion.5), channel_id=1, source_target_pairs={{0,1},{1,0},{2,3},{3,2},{4,5},{5,4},{6,7},{7,6},{8,9},{9,8},{10,11... | collective-permute-start | bytes 3145736 | tf_op jit(solution)/shard_map/ppermute | solution.py:101
  709.0 101.5 %collective-permute-start.27 = (bf16[512,1024]{1,0:T(8,128)(2,1)S(1)}, bf16[512,1024]{1,0:T(8,128)(2,1)S(1)}, u32[]{:S(2)}, u32[]{:S(2)}) collective-permute-start(bf16[512,1024]{1,0:T(8,128)(2,1)S(1)} %dynamic-slice_bitcast_fusion), channel_id=1, source_target_pairs={{0,2},{1,3},{2,0},{3,1},{4,6},{5,7},{6,4},{7,5},{8,10},{9,11},{10,... | collective-permute-start | bytes 3145736 | tf_op jit(solution)/shard_map/ppermute | solution.py:101
  751.6 60.8 %collective-permute-start.23 = (bf16[512,1024]{1,0:T(8,128)(2,1)S(1)}, bf16[512,1024]{1,0:T(8,128)(2,1)S(1)}, u32[]{:S(2)}, u32[]{:S(2)}) collective-permute-start(bf16[512,1024]{1,0:T(8,128)(2,1)S(1)} %dynamic-slice_bitcast_fusion.1), channel_id=1, source_target_pairs={{0,1},{1,0},{2,3},{3,2},{4,5},{5,4},{6,7},{7,6},{8,9},{9,8},{10,11... | collective-permute-start | bytes 3145736 | tf_op jit(solution)/shard_map/ppermute | solution.py:101
  753.7 68.9 %collective-permute-start.20 = (bf16[512,512]{1,0:T(8,128)(2,1)S(1)}, bf16[512,512]{1,0:T(8,128)(2,1)S(1)}, u32[]{:S(2)}, u32[]{:S(2)}) collective-permute-start(bf16[512,512]{1,0:T(8,128)(2,1)S(1)} %dynamic-slice_bitcast_fusion.8), channel_id=1, source_target_pairs={{0,1},{1,0},{2,3},{3,2},{4,5},{5,4},{6,7},{7,6},{8,9},{9,8},{10,11... | collective-permute-start | bytes 1572872 | tf_op jit(solution)/shard_map/ppermute | solution.py:101
  787.5 57.7 %collective-permute-start.16 = (bf16[512,512]{1,0:T(8,128)(2,1)S(1)}, bf16[512,512]{1,0:T(8,128)(2,1)S(1)}, u32[]{:S(2)}, u32[]{:S(2)}) collective-permute-start(bf16[512,512]{1,0:T(8,128)(2,1)S(1)} %dynamic-slice_bitcast_fusion.9), channel_id=1, source_target_pairs={{0,2},{1,3},{2,0},{3,1},{4,6},{5,7},{6,4},{7,5},{8,10},{9,11},{10,... | collective-permute-start | bytes 1572872 | tf_op jit(solution)/shard_map/ppermute | solution.py:101
  822.6 46.8 %collective-permute-start.8 = (bf16[512,512]{1,0:T(8,128)(2,1)S(1)}, bf16[512,512]{1,0:T(8,128)(2,1)S(1)}, u32[]{:S(2)}, u32[]{:S(2)}) collective-permute-start(bf16[512,512]{1,0:T(8,128)(2,1)S(1)} %dynamic-slice_bitcast_fusion.11), channel_id=1, source_target_pairs={{0,2},{1,3},{2,0},{3,1},{4,6},{5,7},{6,4},{7,5},{8,10},{9,11},{10,... | collective-permute-start | bytes 1572872 | tf_op jit(solution)/shard_map/ppermute | solution.py:101
  871.8 56.2 %collective-permute-start.22 = (bf16[1024,512]{1,0:T(8,128)(2,1)S(1)}, bf16[1024,512]{1,0:T(8,128)(2,1)S(1)}, u32[]{:S(2)}, u32[]{:S(2)}) collective-permute-start(bf16[1024,512]{1,0:T(8,128)(2,1)S(1)} %maximum_select_fusion.13), channel_id=1, source_target_pairs={{0,2},{1,3},{2,0},{3,1},{4,6},{5,7},{6,4},{7,5},{8,10},{9,11},{10,... | collective-permute-start | bytes 3145736 | tf_op jit(solution)/shard_map/ppermute | solution.py:105
  880.8 47.9 %collective-permute-start.18 = (bf16[1024,512]{1,0:T(8,128)(2,1)S(1)}, bf16[1024,512]{1,0:T(8,128)(2,1)S(1)}, u32[]{:S(2)}, u32[]{:S(2)}) collective-permute-start(bf16[1024,512]{1,0:T(8,128)(2,1)S(1)} %maximum_select_fusion.12), channel_id=1, source_target_pairs={{0,1},{1,0},{2,3},{3,2},{4,5},{5,4},{6,7},{7,6},{8,9},{9,8},{10,11... | collective-permute-start | bytes 3145736 | tf_op jit(solution)/shard_map/ppermute | solution.py:105
  (81 other events, 1719.7 us)
Sparse Core Ops, SparseCore 0:
  18.5 57.4 all-gather.5
  77.8 35.3 all-gather.7
  118.9 120.1 all-gather.9
  420.1 89.0 reduce-scatter.6
  511.9 87.9 reduce-scatter.4
  620.3 35.7 reduce-scatter.10
  700.6 89.4 reduce-scatter.8
  956.0 64.6 all-reduce.2
